TPU v7x, 32 devices: a whole 2x2x4 slice. The times are simulated.
32 devices in a mesh: gx: 8 (over z, y), gz: 4 (over x, core).
Axes of the slice: x: 2, y: 2, z: 4, core: 2. Of those that a mesh axis runs over, the one named last changes fastest.
Arguments:
- populations: float32 [19, 32, 64, 128], P(None, 'gx', 'gz'), may hold values from 0.005 to 0.5, as said below
- relax_rates: float32 [19], replicated, may hold values from 0.6 to 1.9
- wall_flags: int32 [64, 128], replicated, may hold values 0 or 1
- particles: float32 [4, 8, 4, 2048], P(None, 'gx', 'gz'), may hold values from -2 to 2, as said below
- migrate_list: int32 [8, 4, 4, 128], P('gx', 'gz'), may hold values from -1 to 2047, as said below
- tile_slot: int32 [8, 4, 9, 1024], P('gx', 'gz'), may hold values from -1 to 2559, as said below
- tile_cell: int32 [8, 4, 9, 1024], P('gx', 'gz'), may hold values from 0 to 8191, as said below
- tile_weight: float32 [8, 4, 9, 1024], P('gx', 'gz'), may hold values from 0.1 to 1
Outputs:
- new_populations: float32 [19, 32, 64, 128], P(None, 'gx', 'gz')
Inputs may be any that keep to these rules, and one draw needn't show every extreme that they name: `populations`: each is w_q (1 + 3 c_q.u + 0.25 e) for a node velocity u of small magnitude and e within -1 to 1, so every density lies near 1. `particles`: rows 0 to 2 are velocities, row 3 drag coefficients between 0.2 and 1. `migrate_list`: entry [i, k, d, m] is a slot of device (i, k) or -1; live entries come first in each list, and no slot appears twice among one device's four lists. List d sends to the next device along gx (d = 0), the previous along gx (1), the next along gz (2), the previous along gz (3). A list may be full. `tile_slot`: entry [i, k, j, m] is a slot of that device's resident particles or -1; live entries come first in each bucket, and a bucket may be full. `tile_cell`: bucket j addresses the device j // 3 - 1 steps along gx and j % 3 - 1 along gz; a tile for a device one step along an axis lies in that device's plane of nodes facing the sender along that axis.
All inputs are finite; a program needn't handle non-finite values.
Results may differ from a plain program's by a relative error of at most 0.0003.
Values sent between devices are 32-bit elements; how exact they have to be, the bound alone decides.
A program may use at most 64 MiB of HBM per device.

v0:
```python
import jax
import jax.numpy as jnp
import numpy as np
from jax import lax
from jax.sharding import PartitionSpec as P


def shifted(array, axis, by):
    devices = lax.axis_size(axis)
    return lax.ppermute(array, axis, [(i, (i + by) % devices) for i in range(devices)])


def padded_2(block, sides, width):
    for axis, dim in sides:
        count = lax.axis_size(axis)
        forward = [(i, i + 1) for i in range(count - 1)]
        forward.append((count - 1, 0))
        backward = [(target, source) for source, target in forward]
        low = lax.ppermute(
            lax.slice_in_dim(block, block.shape[dim] - width, None, axis=dim), axis, forward
        )
        high = lax.ppermute(lax.slice_in_dim(block, 0, width, axis=dim), axis, backward)
        block = jnp.concatenate([low, block, high], axis=dim)
    return block


def lattice_velocities():
    return (
        np.array(
            [
                [0, 0, 0],
                [1, 0, 0],
                [-1, 0, 0],
                [0, 1, 0],
                [0, -1, 0],
                [0, 0, 1],
                [0, 0, -1],
                [1, 1, 0],
                [-1, -1, 0],
                [1, -1, 0],
                [-1, 1, 0],
                [1, 0, 1],
                [-1, 0, -1],
                [1, 0, -1],
                [-1, 0, 1],
                [0, 1, 1],
                [0, -1, -1],
                [0, 1, -1],
                [0, -1, 1],
            ]
        )
        * 1.0
    )


def lattice_weights():
    return np.array([1.0 / 3.0] + [1.0 / 18.0] * 6 + [1.0 / 36.0] * 12)


def opposite_table():
    table = lattice_velocities()
    return [int(np.argmax(np.all(table == -entry, axis=1))) for entry in table]


def moment_basis():
    table = lattice_velocities()
    along_x, along_y, along_z = (table[:, 0], table[:, 1], table[:, 2])
    square = along_x * along_x + along_y * along_y + along_z * along_z
    raw_list = [
        np.ones(19),
        square,
        square * square,
        along_x,
        along_y,
        along_z,
        square * along_x,
        square * along_y,
        square * along_z,
        3 * along_x * along_x - square,
        square * (3 * along_x * along_x - square),
        along_y * along_y - along_z * along_z,
        square * (along_y * along_y - along_z * along_z),
        along_x * along_y,
        along_y * along_z,
        along_x * along_z,
        along_x * (along_y * along_y - along_z * along_z),
        along_y * (along_z * along_z - along_x * along_x),
        along_z * (along_x * along_x - along_y * along_y),
    ]
    basis = []
    for vector in raw_list:
        vector = np.array(vector) * 1.0
        for earlier in basis:
            vector = vector - np.dot(vector, earlier) * earlier
        basis.append(vector / np.sqrt(np.dot(vector, vector)))
    return np.stack(basis)


def collision_operator(relax_rates):
    basis = jnp.asarray(moment_basis(), jnp.float32)
    keep_mask = jnp.asarray(np.array([0, 1, 1, 0, 0, 0] + [1] * 13) * 1.0, jnp.float32)
    scaled = relax_rates * keep_mask
    return jnp.dot(basis.T * scaled[None, :], basis, precision=lax.Precision.HIGHEST)


def collide(populations, force_sums, relax_rates):
    highest = lax.Precision.HIGHEST
    velocities = jnp.asarray(lattice_velocities(), jnp.float32)
    weights = jnp.asarray(lattice_weights(), jnp.float32).reshape(19, 1, 1, 1)
    density = jnp.sum(populations, axis=0)
    momentum = jnp.tensordot(velocities.T, populations, axes=1, precision=highest)
    force = force_sums[:3] - force_sums[3] * (momentum / density)
    velocity = (momentum + 0.5 * force) / density
    along_u = jnp.tensordot(velocities, velocity, axes=1, precision=highest)
    along_f = jnp.tensordot(velocities, force, axes=1, precision=highest)
    speed_sq = jnp.sum(velocity * velocity, axis=0)
    u_dot_f = jnp.sum(velocity * force, axis=0)
    equilibrium = (
        weights * density * (1.0 + 3.0 * along_u + 4.5 * along_u * along_u - 1.5 * speed_sq)
    )
    source = weights * (3.0 * along_f - 3.0 * u_dot_f + 9.0 * along_u * along_f)
    departure = populations - equilibrium + 0.5 * source
    relaxed = jnp.tensordot(collision_operator(relax_rates), departure, axes=1, precision=highest)
    return populations + source - relaxed


def shift_wall(field, offset, fill):
    if offset == 0:
        return field
    border = jnp.full_like(field[..., :1], fill)
    if offset == 1:
        return jnp.concatenate([border, field[..., :-1]], axis=-1)
    return jnp.concatenate([field[..., 1:], border], axis=-1)


def solid_nodes(wall_flags):
    depth_y = wall_flags.shape[1]
    height = lax.broadcasted_iota(jnp.int32, wall_flags.shape, 1)
    boundary = (height == 0) | (height == depth_y - 1)
    return jnp.where(boundary, 1, wall_flags)


def pick_columns(table, index):
    taken = jnp.take(table, jnp.maximum(index, 0), axis=1)
    return jnp.where(index >= 0, taken, 0.0)


def depart(own_slots, lists):
    leaving = jnp.stack([pick_columns(own_slots, lists[target]) for target in range(4)])
    flat_list = lists.reshape(-1)
    gone = (
        jnp.zeros((own_slots.shape[1],), jnp.float32)
        .at[jnp.maximum(flat_list, 0)]
        .max((flat_list >= 0).astype(jnp.float32))
    )
    return (own_slots * (1.0 - gone)[None, :], leaving)


def tile_values(resident, slots, weights):
    picked = pick_columns(resident, slots)
    scale = weights * picked[3]
    return jnp.stack([scale * picked[0], scale * picked[1], scale * picked[2], scale])


def body(
    populations, relax_rates, wall_flags, particles, migrate_list, tile_slot, tile_cell, tile_weight
):
    width_x, width_z, depth_y = (populations.shape[1], populations.shape[2], populations.shape[3])
    node_count = width_x * width_z * depth_y
    staying, leaving = depart(particles[:, 0, 0], migrate_list[0, 0])
    arrivals = []
    for target, offset in ((0, 1), (1, -1)):
        arrivals.append(shifted(leaving[target], "gx", offset))
    for target, offset in ((2, 1), (3, -1)):
        arrivals.append(shifted(leaving[target], "gz", offset))
    resident = jnp.concatenate([staying] + arrivals, axis=1)
    values = tile_values(resident, tile_slot[0, 0], tile_weight[0, 0])
    cell_index = tile_cell[0, 0]
    packed = jnp.concatenate([values, cell_index.astype(jnp.float32)[None]], axis=0)
    grouped = packed.reshape(5, 3, 3, -1)
    collected = [grouped[:, 1]]
    for source, offset in ((2, 1), (0, -1)):
        collected.append(shifted(grouped[:, source], "gx", offset))
    merged = jnp.concatenate(collected, axis=2)
    finals = [merged[:, 1]]
    for source, offset in ((2, 1), (0, -1)):
        finals.append(shifted(merged[:, source], "gz", offset))
    arrived = jnp.concatenate(finals, axis=1)
    force_sums = (
        jnp.zeros((4, node_count), jnp.float32).at[:, arrived[4].astype(jnp.int32)].add(arrived[:4])
    )
    force_sums = force_sums.reshape(4, width_x, width_z, depth_y)
    collided = collide(populations, force_sums, relax_rates)
    table = lattice_velocities()
    padded = padded_2(collided, (("gx", 1), ("gz", 2)), 1)
    solid_full = solid_nodes(wall_flags)
    wrapped = jnp.concatenate([solid_full[-1:], solid_full, solid_full[:1]], axis=0)
    solid_near = lax.dynamic_slice_in_dim(wrapped, lax.axis_index("gz") * width_z, width_z + 2, 0)
    opposite = opposite_table()
    outputs = []
    for direction in range(19):
        step_x, step_y, step_z = [int(entry) for entry in table[direction]]
        moved = padded[
            direction, 1 - step_x : 1 - step_x + width_x, 1 - step_z : 1 - step_z + width_z
        ]
        moved = shift_wall(moved, step_y, 0.0)
        blocked = shift_wall(solid_near[1 - step_z : 1 - step_z + width_z], step_y, 1)
        outputs.append(jnp.where(blocked[None] > 0, collided[opposite[direction]], moved))
    return jnp.stack(outputs)


def solution(mesh):
    return jax.shard_map(
        body,
        mesh=mesh,
        in_specs=(
            P(None, "gx", "gz", None),
            P(),
            P(),
            P(None, "gx", "gz", None),
            P("gx", "gz", None, None),
            P("gx", "gz", None, None),
            P("gx", "gz", None, None),
            P("gx", "gz", None, None),
        ),
        out_specs=P(None, "gx", "gz", None),
        check_vma=False,
    )
```

profile of v0, /device:TPU:0, one launch (start us, length us, event | category | flops | bytes accessed | tf_op | source)
XLA Modules:
  0.0 153.5 jit_solution(11391370204902747369)
XLA Ops:
  0.0 0.9 compare_and_fusion
  0.9 0.8 compare_bitcast_fusion
  1.7 1.1 copy.180
  2.8 0.6 gather_fusion.1
  3.5 0.1 bitcast_select_fusion.3
  3.6 3.0 %collective-permute-start = (f32[4,128]{0,1:T(8,128)S(1)}, f32[4,128]{0,1:T(8,128)S(1)}, u32[]{:S(2)}, u32[]{:S(2)}) collective-permute-start(f32[4,128]{0,1:T(8,128)S(1)} %bitcast_select_fusion.3), channel_id=1, source_target_pairs={{0,4},{4,8},{8,12},{12,16},{16,20},{20,24},{24,28},{28,0},{1,5},{5... | collective-permute-start | bytes 6152 | tf_op jit(solution)/shard_map/ppermute | solution.py:10
  6.6 0.6 gather_fusion.2
  7.3 0.1 bitcast_select_fusion.2
  7.4 3.1 %collective-permute-start.1 = (f32[4,128]{0,1:T(8,128)S(1)}, f32[4,128]{0,1:T(8,128)S(1)}, u32[]{:S(2)}, u32[]{:S(2)}) collective-permute-start(f32[4,128]{0,1:T(8,128)S(1)} %bitcast_select_fusion.2), channel_id=1, source_target_pairs={{0,28},{4,0},{8,4},{12,8},{16,12},{20,16},{24,20},{28,24},{1,29},{... | collective-permute-start | bytes 6152 | tf_op jit(solution)/shard_map/ppermute | solution.py:10
  10.5 0.6 gather_fusion.3
  11.1 0.1 bitcast_select_fusion.1
  11.3 0.6 gather_fusion.4
  12.0 0.1 bitcast_select_fusion
  12.1 1.8 %collective-permute-start.3 = (f32[4,128]{0,1:T(8,128)S(1)}, f32[4,128]{0,1:T(8,128)}, u32[]{:S(2)}, u32[]{:S(2)}) collective-permute-start(f32[4,128]{0,1:T(8,128)S(1)} %bitcast_select_fusion), channel_id=1, source_target_pairs={{0,3},{1,0},{2,1},{3,2},{4,7},{5,4},{6,5},{7,6},{8,11},{9,8},{10,9... | collective-permute-start | bytes 6152 | tf_op jit(solution)/shard_map/ppermute | solution.py:10
  14.1 0.6 slice_compare_fusion
  14.7 0.7 fusion.41
  15.4 4.1 %scatter_custom_fusion = f32[2048]{0:T(1024)S(1)} fusion(s32[512]{0:T(512)S(1)} %maximum_bitcast_fusion.4, f32[512]{0:T(512)S(1)} %convert_bitcast_fusion, f32[]{:T(128)} %constant.28.clone.1), kind=kCustom, calls=%fused_computation.155 | custom fusion | flops 512 | bytes 8196 | tf_op jit(solution)/shard_map/scatter-max | solution.py:154
  19.6 0.3 multiply_dynamic-update-slice_fusion
  19.9 0.3 copy-done.9
  20.4 0.7 mul.156
  21.1 1.1 convolution_bitcast_fusion
  22.2 0.8 convert_element_type.35
  23.1 0.8 constant_dynamic-update-slice_fusion
  24.0 31.0 %gather_fusion = f32[9216,4]{1,0:T(8,128)} fusion(f32[4,2560]{0,1:T(8,128)S(1)} %constant_dynamic-update-slice_fusion, s32[9216]{0:T(1024)S(1)} %broadcast_clamp_fusion), kind=kCustom, calls=%fused_computation.4 | custom fusion | bytes 331776 | tf_op jit(solution)/shard_map/jit(_take)/gather | solution.py:144
  55.0 3.1 %copy.181 = f32[9,1024,4]{1,2,0:T(4,128)S(1)} copy(f32[9,1024,4]{2,1,0:T(8,128)} %bitcast.216) | data formatting | bytes 294912 | tf_op jit(solution)/shard_map/jit(_take)/gather | solution.py:144
  58.3 0.4 concatenate.109
  58.8 4.7 %collective-permute-start.5 = (f32[5,3,1024]{2,0,1:T(8,128)S(1)}, f32[5,3,1024]{2,0,1:T(8,128)S(1)}, u32[]{:S(2)}, u32[]{:S(2)}) collective-permute-start(f32[5,3,1024]{2,0,1:T(8,128)S(1)} %get-tuple-element.43), channel_id=1, source_target_pairs={{0,28},{4,0},{8,4},{12,8},{16,12},{20,16},{24,20},{28,24},{1,29},{... | collective-permute-start | bytes 184328 | tf_op jit(solution)/shard_map/ppermute | solution.py:10
  63.6 2.6 %collective-permute-done.4 = f32[5,3,1024]{2,0,1:T(8,128)S(1)} collective-permute-done((f32[5,3,1024]{2,0,1:T(8,128)S(1)}, f32[5,3,1024]{2,0,1:T(8,128)S(1)}, u32[]{:S(2)}, u32[]{:S(2)}) %collective-permute-start.4) | collective-permute-done | bytes 61472 | tf_op jit(solution)/shard_map/ppermute | solution.py:10
  66.4 1.7 %collective-permute-start.7 = (f32[5,3072]{1,0:T(8,128)S(1)}, f32[5,3072]{1,0:T(8,128)S(1)}, u32[]{:S(2)}, u32[]{:S(2)}) collective-permute-start(f32[5,3072]{1,0:T(8,128)S(1)} %get-tuple-element.40), channel_id=1, source_target_pairs={{0,3},{1,0},{2,1},{3,2},{4,7},{5,4},{6,5},{7,6},{8,11},{9,8},{10,9... | collective-permute-start | bytes 184328 | tf_op jit(solution)/shard_map/ppermute | solution.py:10
  68.1 2.3 %collective-permute-done.6 = f32[5,3072]{1,0:T(8,128)S(1)} collective-permute-done((f32[5,3072]{1,0:T(8,128)S(1)}, f32[5,3072]{1,0:T(8,128)S(1)}, u32[]{:S(2)}, u32[]{:S(2)}) %collective-permute-start.6) | collective-permute-done | bytes 61472 | tf_op jit(solution)/shard_map/ppermute | solution.py:10
  70.5 2.9 %copy.182 = f32[9216,4]{1,0:T(8,128)} copy(f32[9216,4]{0,1:T(4,128)S(1)} %fusion.11) | data formatting | bytes 294912 | tf_op jit(solution)/shard_map/slice | solution.py:190
  73.5 51.9 %scatter_custom_fusion.1 = f32[4,8192]{0,1:T(8,128)} fusion(s32[9216]{0:T(1024)S(1)} %bitcast.232, f32[9216,4]{1,0:T(8,128)} %copy.182, f32[]{:T(128)} %constant.28.clone.1), kind=kCustom, calls=%fused_computation.8 | custom fusion | flops 36864 | bytes 131584 | tf_op jit(solution)/shard_map/scatter-add | solution.py:190
  125.4 4.4 %slice_reduce_fusion = f32[8192]{0:T(1024)S(1)} fusion(f32[4,8192]{0,1:T(8,128)} %scatter_custom_fusion.1), kind=kLoop, calls=%fused_computation.7 | loop fusion | bytes 65536 | tf_op jit(solution)/shard_map/slice | solution.py:112
  129.9 2.8 %copy.185 = f32[3,4,16,128]{3,0,2,1:T(4,128)S(1)} copy(f32[3,4,16,128]{0,3,2,1:T(8,128)} %bitcast.215) | data formatting | bytes 196608 | tf_op jit(solution)/shard_map/slice | solution.py:112
  132.7 1.0 multiply_reduce_fusion.1
  133.8 0.9 fusion.42
  134.7 0.9 fusion.43
  135.6 0.4 fusion.10
  136.0 1.1 fusion.2
  137.0 0.4 copy_subtract_fusion
  137.5 4.8 %collective-permute-start.9 = (f32[19,1,16,128]{3,2,1,0:T(8,128)S(1)}, f32[19,1,16,128]{3,2,1,0:T(8,128)S(1)}, u32[]{:S(2)}, u32[]{:S(2)}) collective-permute-start(f32[19,1,16,128]{3,2,1,0:T(8,128)S(1)} %get-tuple-element.37), channel_id=1, source_target_pairs={{4,0},{8,4},{12,8},{16,12},{20,16},{24,20},{28,24},{0,28},{5,1},{9... | collective-permute-start | bytes 466952 | tf_op jit(solution)/shard_map/ppermute | solution.py:22
  142.3 4.1 %collective-permute-done.8 = f32[19,1,16,128]{3,2,1,0:T(8,128)S(1)} collective-permute-done((f32[19,1,16,128]{3,2,1,0:T(8,128)S(1)}, f32[19,1,16,128]{3,2,1,0:T(8,128)S(1)}, u32[]{:S(2)}, u32[]{:S(2)}) %collective-permute-start.8) | collective-permute-done | bytes 155680 | tf_op jit(solution)/shard_map/ppermute | solution.py:19
  146.4 0.9 collective-permute-done.9
  147.6 0.4 collective-permute-start.10
  148.0 1.4 collective-permute-start.11
  149.4 1.9 %collective-permute-done.10 = f32[19,6,1,128]{3,2,1,0:T(1,128)S(1)} collective-permute-done((f32[19,6,1,128]{3,2,1,0:T(1,128)S(1)}, f32[19,6,1,128]{3,2,1,0:T(1,128)S(1)}, u32[]{:S(2)}, u32[]{:S(2)}) %collective-permute-start.10) | collective-permute-done | bytes 58400 | tf_op jit(solution)/shard_map/ppermute | solution.py:19
  152.1 0.8 copy-done.15
  152.9 0.6 constant_dynamic-update-slice_fusion.4
  (100 shorter events, 2.4 us)
Async XLA Ops:
  0.0 13.9 %copy-start.11 = (s32[1,1,4,128]{3,2,1,0:T(4,128)S(1)}, s32[1,1,4,128]{3,2,1,0:T(4,128)}, u32[]{:S(2)}) copy-start(s32[1,1,4,128]{3,2,1,0:T(4,128)} %param.18) | copy-start | bytes 6148
  0.0 13.9 %copy-start.1 = (s32[1,1,9,1024]{3,1,2,0:T(1,128)S(1)}, s32[1,1,9,1024]{3,1,2,0:T(1,128)}, u32[]{:S(2)}) copy-start(s32[1,1,9,1024]{3,1,2,0:T(1,128)} %param.19) | copy-start | bytes 110596
  0.0 14.0 %copy-start.10 = (s32[64,128]{1,0:T(8,128)S(1)}, s32[64,128]{1,0:T(8,128)}, u32[]{:S(2)}) copy-start(s32[64,128]{1,0:T(8,128)} %param.16) | copy-start | bytes 98308
  3.6 19.4 %collective-permute-start = (f32[4,128]{0,1:T(8,128)S(1)}, f32[4,128]{0,1:T(8,128)S(1)}, u32[]{:S(2)}, u32[]{:S(2)}) collective-permute-start(f32[4,128]{0,1:T(8,128)S(1)} %bitcast_select_fusion.3), channel_id=1, source_target_pairs={{0,4},{4,8},{8,12},{12,16},{16,20},{20,24},{24,28},{28,0},{1,5},{5... | collective-permute-start | bytes 6152 | tf_op jit(solution)/shard_map/ppermute | solution.py:10
  7.4 15.7 %collective-permute-start.1 = (f32[4,128]{0,1:T(8,128)S(1)}, f32[4,128]{0,1:T(8,128)S(1)}, u32[]{:S(2)}, u32[]{:S(2)}) collective-permute-start(f32[4,128]{0,1:T(8,128)S(1)} %bitcast_select_fusion.2), channel_id=1, source_target_pairs={{0,28},{4,0},{8,4},{12,8},{16,12},{20,16},{24,20},{28,24},{1,29},{... | collective-permute-start | bytes 6152 | tf_op jit(solution)/shard_map/ppermute | solution.py:10
  11.3 11.8 %collective-permute-start.2 = (f32[4,128]{0,1:T(8,128)S(1)}, f32[4,128]{0,1:T(8,128)S(1)}, u32[]{:S(2)}, u32[]{:S(2)}) collective-permute-start(f32[4,128]{0,1:T(8,128)S(1)} %bitcast_select_fusion.1), channel_id=1, source_target_pairs={{0,1},{1,2},{2,3},{3,0},{4,5},{5,6},{6,7},{7,4},{8,9},{9,10},{10,1... | collective-permute-start | bytes 6152 | tf_op jit(solution)/shard_map/ppermute | solution.py:10
  12.1 11.0 %collective-permute-start.3 = (f32[4,128]{0,1:T(8,128)S(1)}, f32[4,128]{0,1:T(8,128)}, u32[]{:S(2)}, u32[]{:S(2)}) collective-permute-start(f32[4,128]{0,1:T(8,128)S(1)} %bitcast_select_fusion), channel_id=1, source_target_pairs={{0,3},{1,0},{2,1},{3,2},{4,7},{5,4},{6,5},{7,6},{8,11},{9,8},{10,9... | collective-permute-start | bytes 6152 | tf_op jit(solution)/shard_map/ppermute | solution.py:10
  14.1 8.9 %copy-start = (f32[19,4,16,128]{3,2,1,0:T(8,128)S(1)}, f32[19,4,16,128]{3,2,1,0:T(8,128)}, u32[]{:S(2)}) copy-start(f32[19,4,16,128]{3,2,1,0:T(8,128)} %param.14) | copy-start | bytes 1867780
  19.5 0.7 copy-start.9
  19.5 0.8 copy-start.8
  19.5 0.8 copy-start.7
  19.5 2.6 %copy-start.6 = (s32[16,127]{1,0:T(8,128)S(1)}, s32[16,127]{1,0:T(8,128)}, u32[]{:S(2)}) copy-start(s32[16,127]{1,0:T(8,128)} %get-tuple-element.53) | copy-start | bytes 24388
  55.0 3.2 %copy-start.2 = (f32[1,1,9,1024]{3,1,2,0:T(1,128)S(1)}, f32[1,1,9,1024]{3,1,2,0:T(1,128)}, u32[]{:S(2)}) copy-start(f32[1,1,9,1024]{3,1,2,0:T(1,128)} %param.21) | copy-start | bytes 110596
  58.1 5.5 %copy-start.5 = (s32[16,127]{1,0:T(8,128)S(1)}, s32[16,127]{1,0:T(8,128)}, u32[]{:S(2)}) copy-start(s32[16,127]{1,0:T(8,128)} %get-tuple-element.52) | copy-start | bytes 24388
  58.2 9.9 %copy-start.4 = (s32[16,127]{1,0:T(8,128)S(1)}, s32[16,127]{1,0:T(8,128)}, u32[]{:S(2)}) copy-start(s32[16,127]{1,0:T(8,128)} %get-tuple-element.51) | copy-start | bytes 24388
  58.7 7.5 %collective-permute-start.4 = (f32[5,3,1024]{2,0,1:T(8,128)S(1)}, f32[5,3,1024]{2,0,1:T(8,128)S(1)}, u32[]{:S(2)}, u32[]{:S(2)}) collective-permute-start(f32[5,3,1024]{2,0,1:T(8,128)S(1)} %get-tuple-element.44), channel_id=1, source_target_pairs={{0,4},{4,8},{8,12},{12,16},{16,20},{20,24},{24,28},{28,0},{1,5},{5... | collective-permute-start | bytes 184328 | tf_op jit(solution)/shard_map/ppermute | solution.py:10
  58.8 7.4 %collective-permute-start.5 = (f32[5,3,1024]{2,0,1:T(8,128)S(1)}, f32[5,3,1024]{2,0,1:T(8,128)S(1)}, u32[]{:S(2)}, u32[]{:S(2)}) collective-permute-start(f32[5,3,1024]{2,0,1:T(8,128)S(1)} %get-tuple-element.43), channel_id=1, source_target_pairs={{0,28},{4,0},{8,4},{12,8},{16,12},{20,16},{24,20},{28,24},{1,29},{... | collective-permute-start | bytes 184328 | tf_op jit(solution)/shard_map/ppermute | solution.py:10
  66.3 4.1 %collective-permute-start.6 = (f32[5,3072]{1,0:T(8,128)S(1)}, f32[5,3072]{1,0:T(8,128)S(1)}, u32[]{:S(2)}, u32[]{:S(2)}) collective-permute-start(f32[5,3072]{1,0:T(8,128)S(1)} %get-tuple-element.41), channel_id=1, source_target_pairs={{0,1},{1,2},{2,3},{3,0},{4,5},{5,6},{6,7},{7,4},{8,9},{9,10},{10,1... | collective-permute-start | bytes 184328 | tf_op jit(solution)/shard_map/ppermute | solution.py:10
  66.4 4.1 %collective-permute-start.7 = (f32[5,3072]{1,0:T(8,128)S(1)}, f32[5,3072]{1,0:T(8,128)S(1)}, u32[]{:S(2)}, u32[]{:S(2)}) collective-permute-start(f32[5,3072]{1,0:T(8,128)S(1)} %get-tuple-element.40), channel_id=1, source_target_pairs={{0,3},{1,0},{2,1},{3,2},{4,7},{5,4},{6,5},{7,6},{8,11},{9,8},{10,9... | collective-permute-start | bytes 184328 | tf_op jit(solution)/shard_map/ppermute | solution.py:10
  129.9 2.9 %copy-start.13 = (f32[19,3,1,1]{0,1,3,2:T(4,128)S(1)}, f32[19,3,1,1]{0,1,3,2:T(4,128)}, u32[]{:S(2)}) copy-start(f32[19,3,1,1]{0,1,3,2:T(4,128)} %constant.121) | copy-start | bytes 688
  133.8 1.8 %copy-start.14 = (f32[19]{0:T(128)S(1)}, f32[19]{0:T(128)}, u32[]{:S(2)}) copy-start(f32[19]{0:T(128)} %constant.45.clone) | copy-start | bytes 232
  137.0 9.4 %copy-start.12 = (pred[16,128]{1,0:T(8,128)(4,1)S(1)}, pred[16,128]{1,0:T(8,128)(4,1)}, u32[]{:S(2)}) copy-start(pred[16,128]{1,0:T(8,128)(4,1)} %get-tuple-element.59) | copy-start | bytes 6148
  137.5 8.9 %collective-permute-start.8 = (f32[19,1,16,128]{3,2,1,0:T(8,128)S(1)}, f32[19,1,16,128]{3,2,1,0:T(8,128)S(1)}, u32[]{:S(2)}, u32[]{:S(2)}) collective-permute-start(f32[19,1,16,128]{3,2,1,0:T(8,128)S(1)} %get-tuple-element.38), channel_id=1, source_target_pairs={{0,4},{4,8},{8,12},{12,16},{16,20},{20,24},{24,28},{28,0},{1,5},{5... | collective-permute-start | bytes 466952 | tf_op jit(solution)/shard_map/ppermute | solution.py:19
  137.5 9.8 %collective-permute-start.9 = (f32[19,1,16,128]{3,2,1,0:T(8,128)S(1)}, f32[19,1,16,128]{3,2,1,0:T(8,128)S(1)}, u32[]{:S(2)}, u32[]{:S(2)}) collective-permute-start(f32[19,1,16,128]{3,2,1,0:T(8,128)S(1)} %get-tuple-element.37), channel_id=1, source_target_pairs={{4,0},{8,4},{12,8},{16,12},{20,16},{24,20},{28,24},{0,28},{5,1},{9... | collective-permute-start | bytes 466952 | tf_op jit(solution)/shard_map/ppermute | solution.py:22
  147.3 3.9 %copy-start.3 = (pred[16,128]{1,0:T(8,128)(4,1)S(1)}, pred[16,128]{1,0:T(8,128)(4,1)}, u32[]{:S(2)}) copy-start(pred[16,128]{1,0:T(8,128)(4,1)} %get-tuple-element.57) | copy-start | bytes 6148
  147.6 3.7 %collective-permute-start.10 = (f32[19,6,1,128]{3,2,1,0:T(1,128)S(1)}, f32[19,6,1,128]{3,2,1,0:T(1,128)S(1)}, u32[]{:S(2)}, u32[]{:S(2)}) collective-permute-start(f32[19,6,1,128]{3,2,1,0:T(1,128)S(1)} %get-tuple-element.27), channel_id=1, source_target_pairs={{0,1},{1,2},{2,3},{3,0},{4,5},{5,6},{6,7},{7,4},{8,9},{9,10},{10,1... | collective-permute-start | bytes 175112 | tf_op jit(solution)/shard_map/ppermute | solution.py:19
  148.0 3.3 %collective-permute-start.11 = (f32[19,6,1,128]{3,2,1,0:T(1,128)S(1)}, f32[19,6,1,128]{3,2,1,0:T(1,128)S(1)}, u32[]{:S(2)}, u32[]{:S(2)}) collective-permute-start(f32[19,6,1,128]{3,2,1,0:T(1,128)S(1)} %get-tuple-element.26), channel_id=1, source_target_pairs={{1,0},{2,1},{3,2},{0,3},{5,4},{6,5},{7,6},{4,7},{9,8},{10,9},{11,1... | collective-permute-start | bytes 175112 | tf_op jit(solution)/shard_map/ppermute | solution.py:22
  152.1 0.8 copy-start.15
where the time goes:
time: 155 us; the launch traced here: 154 us
  other arithmetic  63.5 us (41%)
  local copies, waits for them, and re-layouts  51.5 us (33%)
  starting transfers between devices  21.2 us (14%)
  waiting for transfers between devices  11.8 us (8%)
  matrix products  4.86 us (3%)
    scatter-add x1, other arithmetic, body(): jnp.zeros((4, node_count), jnp.float32).at[:, arrived[4].astype(jnp.int32)]  51.9 us
    gather x6, local copies, waits for them, and re-layouts, pick_columns(): taken = jnp.take(table, jnp.maximum(index, 0), axis=1)  36.7 us
    ppermute x8, starting transfers between devices, shifted(): lax.ppermute(array, axis, [(i, (i + by) % devices) for i in range(devices)])  14.5 us
    slice x2, local copies, waits for them, and re-layouts, collide(): force = force_sums[:3] - force_sums[3] * (momentum / density)  7.29 us
    ppermute x2, starting transfers between devices, padded_2(): lax.ppermute(lax.slice_in_dim(block, 0, width, axis=dim), axis, backward)  6.19 us
    ppermute x2, waiting for transfers between devices, padded_2(): lax.ppermute(lax.slice_in_dim(block, block.shape[dim] - width, None, axis...  5.94 us
    ppermute x8, waiting for transfers between devices, shifted(): lax.ppermute(array, axis, [(i, (i + by) % devices) for i in range(devices)])  5 us
    another operation x1, other arithmetic, depart(): gone = jnp.zeros((own_slots.shape[1],), jnp.float32).at[jnp.maximum(flat_...  4.09 us
  transfers between devices with their start and end apart: 12, of which 6 were waited for; matrix products, arithmetic and copies ran while one was open for 7% of the time, Pallas kernels for 0%

commit v1 on v0

v1 whole, which is shorter than its diff:
```python
import jax
import jax.numpy as jnp
import numpy as np
from jax import lax
from jax.experimental import pallas as pl
from jax.experimental.pallas import tpu as pltpu
from jax.sharding import PartitionSpec as P

MESH = pl.DeviceIdType.MESH
VELOCITIES = [
    (0, 0, 0),
    (1, 0, 0),
    (-1, 0, 0),
    (0, 1, 0),
    (0, -1, 0),
    (0, 0, 1),
    (0, 0, -1),
    (1, 1, 0),
    (-1, -1, 0),
    (1, -1, 0),
    (-1, 1, 0),
    (1, 0, 1),
    (-1, 0, -1),
    (1, 0, -1),
    (-1, 0, 1),
    (0, 1, 1),
    (0, -1, -1),
    (0, 1, -1),
    (0, -1, 1),
]
WEIGHTS = [1.0 / 3.0] + [1.0 / 18.0] * 6 + [1.0 / 36.0] * 12
OPPOSITE = [VELOCITIES.index((-a, -b, -c)) for a, b, c in VELOCITIES]
PAIRS = [(q, OPPOSITE[q]) for q in range(1, 19) if q < OPPOSITE[q]]
ALONG_X = [[q for q in range(19) if VELOCITIES[q][0] == s] for s in (1, -1)]
ALONG_Z = [[q for q in range(19) if VELOCITIES[q][2] == s] for s in (1, -1)]
STEP = (1, -1)
CORNERS = [(0, 0), (0, 1), (1, 0), (1, 1)]
PAD = 8


def moment_basis():
    table = np.array(VELOCITIES) * 1.0
    x, y, z = table[:, 0], table[:, 1], table[:, 2]
    square = x * x + y * y + z * z
    raw_list = [
        np.ones(19),
        square,
        square * square,
        x,
        y,
        z,
        square * x,
        square * y,
        square * z,
        3 * x * x - square,
        square * (3 * x * x - square),
        y * y - z * z,
        square * (y * y - z * z),
        x * y,
        y * z,
        x * z,
        x * (y * y - z * z),
        y * (z * z - x * x),
        z * (x * x - y * y),
    ]
    basis = []
    for vector in raw_list:
        for earlier in basis:
            vector = vector - np.dot(vector, earlier) * earlier
        basis.append(vector / np.sqrt(np.dot(vector, vector)))
    return np.stack(basis)


BASIS = moment_basis()
EVEN = [1, 2, 9, 10, 11, 12, 13, 14, 15]
ODD = [6, 7, 8, 16, 17, 18]


def combine(coefficients, values):
    groups = {}
    for coefficient, value in zip(coefficients, values):
        if abs(coefficient) < 1e-9:
            continue
        groups.setdefault(round(abs(coefficient), 9), []).append((float(coefficient), value))
    total = None
    for members in groups.values():
        size = abs(members[0][0])
        lead = 1.0 if members[0][0] > 0 else -1.0
        part = members[0][1]
        for coefficient, value in members[1:]:
            part = part + value if coefficient * lead > 0 else part - value
        if total is None:
            total = part * (size * lead)
        else:
            total = total + part * (size * lead)
    return total


def collide(pops, forces, rates, wanted):
    sums = [pops[a] + pops[b] for a, b in PAIRS]
    gaps = [pops[a] - pops[b] for a, b in PAIRS]
    density = pops[0]
    for entry in sums:
        density = density + entry
    momentum = [
        combine([VELOCITIES[a][axis] for a, _ in PAIRS], gaps) for axis in range(3)
    ]
    inverse = 1.0 / density
    force = [forces[axis] - forces[3] * (momentum[axis] * inverse) for axis in range(3)]
    velocity = [(momentum[axis] + 0.5 * force[axis]) * inverse for axis in range(3)]
    speed_sq = velocity[0] * velocity[0] + velocity[1] * velocity[1] + velocity[2] * velocity[2]
    u_dot_f = velocity[0] * force[0] + velocity[1] * force[1] + velocity[2] * force[2]
    base = 1.0 - 1.5 * speed_sq
    density_odd = 6.0 * density
    rest_source = (-3.0 * WEIGHTS[0]) * u_dot_f
    rest = pops[0] - WEIGHTS[0] * (density * base) + 0.5 * rest_source
    even_in, odd_in, even_source, odd_source = [rest], [], [], []
    for index, (a, _) in enumerate(PAIRS):
        along_u = combine(VELOCITIES[a], velocity)
        along_f = combine(VELOCITIES[a], force)
        weight = WEIGHTS[a]
        source_even = weight * (9.0 * along_u * along_f - 3.0 * u_dot_f)
        source_odd = (3.0 * weight) * along_f
        even_in.append(
            sums[index]
            - (2.0 * weight) * (density * (base + 4.5 * along_u * along_u))
            + source_even
        )
        odd_in.append(gaps[index] - weight * (density_odd * along_u) + source_odd)
        even_source.append(source_even)
        odd_source.append(source_odd)
    firsts = [a for a, _ in PAIRS]
    even_m = [rates[k] * combine(BASIS[k][[0] + firsts], even_in) for k in EVEN]
    odd_m = [rates[k] * combine(BASIS[k][firsts], odd_in) for k in ODD]
    out = {}
    if 0 in wanted:
        out[0] = pops[0] + rest_source - combine(BASIS[EVEN, 0], even_m)
    for index, (a, b) in enumerate(PAIRS):
        if a not in wanted and b not in wanted:
            continue
        even = even_source[index] - combine(BASIS[EVEN, a], even_m)
        odd = odd_source[index] - combine(BASIS[ODD, a], odd_m)
        out[a] = pops[a] + even + odd
        out[b] = pops[b] + even - odd
    return out


def lane_pick(row, lanes):
    table = jnp.broadcast_to(row, lanes.shape)
    return jnp.take_along_axis(table, lanes, axis=1, mode="promise_in_bounds")


def spread(values, rows, lanes, count):
    highs = [v.astype(jnp.bfloat16).astype(jnp.float32) for v in values]
    parts = highs + [v - h for v, h in zip(values, highs)]
    row_iota = lax.broadcasted_iota(jnp.int32, (count, 128), 0)
    lane_iota = lax.broadcasted_iota(jnp.int32, (128, 128), 0)
    left, right = [], []
    for s in range(8):
        hit = row_iota == rows[s : s + 1]
        left.append(
            jnp.concatenate(
                [jnp.where(hit, part[s : s + 1], 0.0) for part in parts], axis=0
            ).astype(jnp.bfloat16)
        )
        right.append(jnp.where(lane_iota == lanes[s : s + 1], 1.0, 0.0).astype(jnp.bfloat16))
    both = lax.dot_general(
        jnp.concatenate(left, axis=1),
        jnp.concatenate(right, axis=1),
        (((1,), (1,)), ((), ())),
        preferred_element_type=jnp.float32,
    )
    return both[: 4 * count] + both[4 * count :]


def kernel(
    devices_x,
    devices_z,
    pops_ref,
    rates_ref,
    wall_ref,
    part_ref,
    list_ref,
    slot_ref,
    cell_ref,
    weight_ref,
    out_ref,
    stay,
    leave,
    arrive,
    values,
    force,
    plane_out,
    plane_in,
    edge_out,
    edge_in,
    corner_in,
    coll,
    halo_x_out,
    halo_x_in,
    halo_z_out,
    halo_z_in,
    halo_c_in,
    solid,
    send_sem,
    recv_sem,
):
    me_x, me_z = lax.axis_index("gx"), lax.axis_index("gz")
    depth_z = 16
    rows_z = wall_ref.shape[0]

    def peer(step_x, step_z):
        return (
            lax.rem(me_x + step_x + devices_x, devices_x),
            lax.rem(me_z + step_z + devices_z, devices_z),
        )

    barrier = pltpu.get_barrier_semaphore()
    around = [(a, b) for a in (-1, 0, 1) for b in (-1, 0, 1) if (a, b) != (0, 0)]
    for step in around:
        pl.semaphore_signal(barrier, inc=1, device_id=peer(*step), device_id_type=MESH)

    count = [0]

    def send(source, target, step):
        at = count[0]
        count[0] += 1
        copy = pltpu.make_async_remote_copy(
            src_ref=source,
            dst_ref=target,
            send_sem=send_sem.at[at],
            recv_sem=recv_sem.at[at],
            device_id=peer(*step),
            device_id_type=MESH,
        )
        copy.start()
        return copy

    lists = list_ref[...]
    lists8 = jnp.concatenate([lists, lists], axis=0)
    list_hi, list_lo = lists8 >> 7, lists8 & 127
    picked = [jnp.zeros((8, 128), jnp.float32) for _ in range(4)]
    for h in range(16):
        hit = list_hi == h
        for c in range(4):
            picked[c] = jnp.where(
                hit, lane_pick(part_ref[c * 16 + h : c * 16 + h + 1], list_lo), picked[c]
            )
    for c in range(4):
        for d in range(4):
            leave[d, c : c + 1, :] = picked[c][d : d + 1]
    pl.semaphore_wait(barrier, len(around))
    migrations = [
        send(leave.at[d], arrive.at[d], step)
        for d, step in enumerate([(1, 0), (-1, 0), (0, 1), (0, -1)])
    ]

    hi_iota = lax.broadcasted_iota(jnp.int32, (16, 128), 0)
    lo_iota = lax.broadcasted_iota(jnp.int32, (128, 128), 0)
    left = jnp.concatenate(
        [jnp.where(hi_iota == list_hi[d : d + 1], 1.0, 0.0) for d in range(4)], axis=1
    ).astype(jnp.bfloat16)
    right = jnp.concatenate(
        [jnp.where(lo_iota == list_lo[d : d + 1], 1.0, 0.0) for d in range(4)], axis=1
    ).astype(jnp.bfloat16)
    gone = lax.dot_general(
        left, right, (((1,), (1,)), ((), ())), preferred_element_type=jnp.float32
    )
    for c in range(4):
        stay[c] = jnp.where(gone > 0.5, 0.0, part_ref[c * 16 : c * 16 + 16])

    def first_pick(j, carry):
        at = pl.ds(pl.multiple_of(j * 8, 8), 8)
        slots = slot_ref[at]
        hi, lo = slots >> 7, slots & 127
        got = [jnp.zeros((8, 128), jnp.float32) for _ in range(4)]
        for h in range(16):
            hit = hi == h
            for c in range(4):
                got[c] = jnp.where(hit, lane_pick(stay[c, h : h + 1], lo), got[c])
        for c in range(4):
            values[c, at] = got[c]
        return carry

    lax.fori_loop(0, 9, first_pick, 0)

    wall = jnp.where(
        (lax.broadcasted_iota(jnp.int32, (depth_z, 128), 1) == 0)
        | (lax.broadcasted_iota(jnp.int32, (depth_z, 128), 1) == 127),
        1,
        wall_ref[pl.ds(pl.multiple_of(me_z * depth_z, depth_z), depth_z)],
    )
    solid[PAD : PAD + depth_z] = wall
    lane = lax.broadcasted_iota(jnp.int32, (1, 128), 1)
    ends = (lane == 0) | (lane == 127)
    below = lax.rem(me_z * depth_z + rows_z - 1, rows_z)
    above = lax.rem(me_z * depth_z + depth_z, rows_z)
    solid[PAD - 1 : PAD] = jnp.where(ends, 1, wall_ref[pl.ds(below, 1)])
    solid[PAD + depth_z : PAD + depth_z + 1] = jnp.where(ends, 1, wall_ref[pl.ds(above, 1)])

    for copy in migrations:
        copy.wait()

    def second_pick(j, carry):
        at = pl.ds(pl.multiple_of(j * 8, 8), 8)
        slots = slot_ref[at]
        hi, lo = slots >> 7, slots & 127
        got = [values[c, at] for c in range(4)]
        for d in range(4):
            hit = hi == 16 + d
            for c in range(4):
                got[c] = jnp.where(hit, lane_pick(arrive[d, c : c + 1], lo), got[c])
        scale = weight_ref[at] * got[3]
        for c in range(3):
            values[c, at] = scale * got[c]
        values[3, at] = scale
        return carry

    lax.fori_loop(0, 9, second_pick, 0)

    def bucket(step_x, step_z):
        at = ((step_x + 1) * 3 + step_z + 1) * 8
        cells = cell_ref[at : at + 8]
        return [values[c, at : at + 8] for c in range(4)], cells

    exchanges = []
    for s, step in enumerate(STEP):
        got, cells = bucket(step, 0)
        plane_out[s] = spread(got, (cells >> 7) & 15, cells & 127, 16).reshape(4, 16, 128)
        exchanges.append(send(plane_out.at[s], plane_in.at[s], (step, 0)))
    for s, step in enumerate(STEP):
        total = None
        for step_x in (-1, 0, 1):
            got, cells = bucket(step_x, step)
            rows = (cells >> 11) + 1 if step_x == 0 else jnp.full_like(cells, 0 if step_x < 0 else 5)
            part = spread(got, rows, cells & 127, 8)
            total = part if total is None else total + part
        edge_out[s] = total.reshape(4, 8, 128)
        exchanges.append(send(edge_out.at[s], edge_in.at[s], (0, step)))
        for sx, step_x in enumerate(STEP):
            exchanges.append(send(edge_out.at[s], corner_in.at[s * 2 + sx], (step_x, step)))
    got, cells = bucket(0, 0)
    force[...] = spread(got, cells >> 7, cells & 127, 64).reshape(4, 4, 16, 128)
    for copy in exchanges:
        copy.wait()
    for s in range(2):
        x = 0 if s == 0 else 3
        for c in range(4):
            force[c, x] = force[c, x] + plane_in[s, c]
    for s in range(2):
        z = 0 if s == 0 else 15
        for c in range(4):
            for x in range(4):
                row = edge_in[s, c, x + 1 : x + 2]
                if x == 0:
                    row = row + corner_in[s * 2, c, 5:6]
                if x == 3:
                    row = row + corner_in[s * 2 + 1, c, 0:1]
                force[c, x, z : z + 1] = force[c, x, z : z + 1] + row

    rates = [rates_ref[k] for k in range(19)]
    halos = []
    for x in (3, 0, 1, 2):
        done = collide(
            [pops_ref[q, x] for q in range(19)],
            [force[c, x] for c in range(4)],
            rates,
            range(19),
        )
        for q in range(19):
            coll[q, 1 + x, PAD : PAD + 16] = done[q]
        for s in range(2):
            z = 15 if s == 0 else 0
            for n, q in enumerate(ALONG_Z[s]):
                halo_z_out[s, n, x : x + 1] = done[q][z : z + 1]
        if x in (3, 0):
            s = 0 if x == 3 else 1
            for n, q in enumerate(ALONG_X[s]):
                halo_x_out[s, n] = done[q]
            halos.append(send(halo_x_out.at[s], halo_x_in.at[s], (STEP[s], 0)))
    for s in range(2):
        halos.append(send(halo_z_out.at[s], halo_z_in.at[s], (0, STEP[s])))
        for sx in range(2):
            q = VELOCITIES.index((STEP[sx], 0, STEP[s]))
            n = ALONG_Z[s].index(q)
            halos.append(
                send(halo_z_out.at[s, n], halo_c_in.at[s * 2 + sx], (STEP[sx], STEP[s]))
            )
    for copy in halos:
        copy.wait()
    for s in range(2):
        for n, q in enumerate(ALONG_X[s]):
            coll[q, 0 if s == 0 else 5, PAD : PAD + 16] = halo_x_in[s, n]
        z = PAD - 1 if s == 0 else PAD + 16
        for n, q in enumerate(ALONG_Z[s]):
            for x in range(4):
                coll[q, 1 + x, z : z + 1] = halo_z_in[s, n, x : x + 1]
        for sx in range(2):
            q = VELOCITIES.index((STEP[sx], 0, STEP[s]))
            x = 3 if sx == 0 else 0
            coll[q, 0 if sx == 0 else 5, z : z + 1] = halo_c_in[s * 2 + sx, x : x + 1]

    for q in range(19):
        step_x, step_y, step_z = VELOCITIES[q]
        blocked = solid[PAD - step_z : PAD - step_z + 16]
        if step_y:
            blocked = pltpu.roll(blocked, step_y % 128, 1)
        for x in range(4):
            moved = coll[q, 1 + x - step_x, PAD - step_z : PAD - step_z + 16]
            if step_y:
                moved = pltpu.roll(moved, step_y % 128, 1)
            out_ref[q, x] = jnp.where(
                blocked > 0, coll[OPPOSITE[q], 1 + x, PAD : PAD + 16], moved
            )


def solution(mesh):
    devices_x, devices_z = mesh.shape["gx"], mesh.shape["gz"]

    def body(pops, rates, wall, particles, lists, slot, cell, weight):
        vmem = pl.BlockSpec(memory_space=pltpu.VMEM)
        smem = pl.BlockSpec(memory_space=pltpu.SMEM)
        f32 = jnp.float32
        return pl.pallas_call(
            lambda *refs: kernel(devices_x, devices_z, *refs),
            out_shape=jax.ShapeDtypeStruct(pops.shape, f32),
            in_specs=[vmem, smem] + [vmem] * 6,
            out_specs=vmem,
            scratch_shapes=[
                pltpu.VMEM((4, 16, 128), f32),
                pltpu.VMEM((4, 8, 128), f32),
                pltpu.VMEM((4, 8, 128), f32),
                pltpu.VMEM((4, 72, 128), f32),
                pltpu.VMEM((4, 4, 16, 128), f32),
                pltpu.VMEM((2, 4, 16, 128), f32),
                pltpu.VMEM((2, 4, 16, 128), f32),
                pltpu.VMEM((2, 4, 8, 128), f32),
                pltpu.VMEM((2, 4, 8, 128), f32),
                pltpu.VMEM((4, 4, 8, 128), f32),
                pltpu.VMEM((19, 6, 32, 128), f32),
                pltpu.VMEM((2, 5, 16, 128), f32),
                pltpu.VMEM((2, 5, 16, 128), f32),
                pltpu.VMEM((2, 5, 8, 128), f32),
                pltpu.VMEM((2, 5, 8, 128), f32),
                pltpu.VMEM((4, 8, 128), f32),
                pltpu.VMEM((32, 128), jnp.int32),
                pltpu.SemaphoreType.DMA((20,)),
                pltpu.SemaphoreType.DMA((20,)),
            ],
            compiler_params=pltpu.CompilerParams(
                collective_id=0, has_side_effects=True, vmem_limit_bytes=48 * 1024 * 1024
            ),
        )(
            pops,
            rates,
            wall,
            particles.reshape(64, 128),
            lists.reshape(4, 128),
            slot.reshape(72, 128),
            cell.reshape(72, 128),
            weight.reshape(72, 128),
        )

    return jax.shard_map(
        body,
        mesh=mesh,
        in_specs=(
            P(None, "gx", "gz", None),
            P(),
            P(),
            P(None, "gx", "gz", None),
            P("gx", "gz", None, None),
            P("gx", "gz", None, None),
            P("gx", "gz", None, None),
            P("gx", "gz", None, None),
        ),
        out_specs=P(None, "gx", "gz", None),
        check_vma=False,
    )
```

time: 155 us -> 28.2 us (0.18)
  other arithmetic: 63.5 us -> 0 us
  local copies, waits for them, and re-layouts: 51.5 us -> 6.4 us
  Pallas kernels: 0 us -> 21.3 us
  starting transfers between devices: 21.2 us -> 0 us
  waiting for transfers between devices: 11.8 us -> 0 us
  matrix products: 4.86 us -> 0 us
    scatter-add x1 -> x0, other arithmetic: 51.9 us -> none  [body(): jnp.zeros((4, node_count), jnp.float32).at[:, arrived[4].astype(jnp.int32)]]
    gather x6 -> x0, local copies, waits for them, and re-layouts: 36.7 us -> none  [pick_columns(): taken = jnp.take(table, jnp.maximum(index, 0), axis=1)]
    pallas_call x0 -> x1, Pallas kernels: none -> 21.3 us  [body(): pl.pallas_call(lambda *refs: kernel(devices_x, devices_z, *refs), out_sha...]
    ppermute x12 -> x0, starting transfers between devices: 21.2 us -> none  [the longest x8 14.5 us: shifted(): lax.ppermute(array, axis, [(i, (i + by) % devices) for i in range(devices)])]
    ppermute x12 -> x0, waiting for transfers between devices: 11.8 us -> none  [the longest x2 5.94 us: padded_2(): lax.ppermute(lax.slice_in_dim(block, block.shape[dim] - width, None, axis...]
    slice x11 -> x0, local copies, waits for them, and re-layouts: 11.3 us -> none  [the longest x2 7.29 us: collide(): force = force_sums[:3] - force_sums[3] * (momentum / density)]
    dot_general x5 -> x0, matrix products: 4.86 us -> none  [the longest x1 1.06 us: collision_operator(): jnp.dot(basis.T * scaled[None, :], basis, precision=lax.Precision.HIGHEST)]
    another operation x2 -> x0, other arithmetic: 4.71 us -> none  [the longest x1 4.09 us: depart(): gone = jnp.zeros((own_slots.shape[1],), jnp.float32).at[jnp.maximum(flat_...]
  transfers between devices with their start and end apart: 12 -> 0, of which waited for: 6 -> 0; matrix products, arithmetic and copies ran while one was open for 7% -> 0% of each run, Pallas kernels for 0% -> 0%
where the time goes in v1:
time: 28.2 us; the launch traced here: 27.7 us
  Pallas kernels  21.3 us (76%)
  local copies, waits for them, and re-layouts  6.4 us (23%)
    pallas_call x1, Pallas kernels, body(): pl.pallas_call(lambda *refs: kernel(devices_x, devices_z, *refs), out_sha...  21.3 us
    unnamed x17, local copies, waits for them, and re-layouts  6.4 us

profile of v1, /device:TPU:0, one launch (start us, length us, event | category | flops | bytes accessed | tf_op | source)
XLA Modules:
  0.0 27.7 jit_solution(7571695259371432885)
XLA Ops:
  0.0 0.0 copy-start.6
  0.0 0.0 copy-start.7
  0.0 0.7 %copy-done.6 = s32[1,1,4,128]{3,2,1,0:T(4,128)S(1)} copy-done((s32[1,1,4,128]{3,2,1,0:T(4,128)S(1)}, s32[1,1,4,128]{3,2,1,0:T(4,128)}, u32[]{:S(2)}) %copy-start.6) | copy-done | bytes 2072
  0.7 0.0 copy-done.7
  0.7 0.0 copy-start
  0.7 1.1 %copy-done = f32[19,4,16,128]{3,2,1,0:T(8,128)S(1)} copy-done((f32[19,4,16,128]{3,2,1,0:T(8,128)S(1)}, f32[19,4,16,128]{3,2,1,0:T(8,128)}, u32[]{:S(2)}) %copy-start) | copy-done | bytes 622616
  1.8 0.0 copy-start.1
  1.8 0.8 %copy-done.1 = s32[1,1,9,1024]{3,1,2,0:T(1,128)S(1)} copy-done((s32[1,1,9,1024]{3,1,2,0:T(1,128)S(1)}, s32[1,1,9,1024]{3,1,2,0:T(1,128)}, u32[]{:S(2)}) %copy-start.1) | copy-done | bytes 36888
  2.5 0.0 copy-start.2
  2.5 0.8 %copy-done.2 = s32[1,1,9,1024]{3,1,2,0:T(1,128)S(1)} copy-done((s32[1,1,9,1024]{3,1,2,0:T(1,128)S(1)}, s32[1,1,9,1024]{3,1,2,0:T(1,128)}, u32[]{:S(2)}) %copy-start.2) | copy-done | bytes 36888
  3.3 0.0 copy-start.3
  3.3 0.8 %copy-done.3 = f32[1,1,9,1024]{3,1,2,0:T(1,128)S(1)} copy-done((f32[1,1,9,1024]{3,1,2,0:T(1,128)S(1)}, f32[1,1,9,1024]{3,1,2,0:T(1,128)}, u32[]{:S(2)}) %copy-start.3) | copy-done | bytes 36888
  4.1 0.0 copy-start.4
  4.1 0.8 %copy-done.4 = s32[64,128]{1,0:T(8,128)S(1)} copy-done((s32[64,128]{1,0:T(8,128)S(1)}, s32[64,128]{1,0:T(8,128)}, u32[]{:S(2)}) %copy-start.4) | copy-done | bytes 32792
  4.8 0.0 copy-start.5
  4.8 0.8 %copy-done.5 = f32[4,1,1,2048]{3,2,1,0:T(1,128)S(1)} copy-done((f32[4,1,1,2048]{3,2,1,0:T(1,128)S(1)}, f32[4,1,1,2048]{3,2,1,0:T(1,128)}, u32[]{:S(2)}) %copy-start.5) | copy-done | bytes 32792
  5.6 21.3 %shard_map.82 = f32[19,4,16,128]{3,2,1,0:T(8,128)S(1)} custom-call(f32[19,4,16,128]{3,2,1,0:T(8,128)S(1)} %copy-done, f32[19]{0:T(128)S(1)} %copy-done.7, s32[64,128]{1,0:T(8,128)S(1)} %copy-done.4, f32[64,128]{1,0:T(8,128)S(1)} %bitcast.8, s32[4,128]{1,0:T(4,128)S(1)} %bitcast.9, s32[72,128]{1,0:T(8,128)S(1)} %bitcast.5, s32[72,128]{1,0:T(8,128)S(1)} %bitcast.6, ...), custom_call_target="tpu_custom_call" | custom-call | tf_op jit(solution)/shard_map/pallas_call | solution.py:424
  26.9 0.8 %copy.10 = f32[19,4,16,128]{3,2,1,0:T(8,128)} copy(f32[19,4,16,128]{3,2,1,0:T(8,128)S(1)} %shard_map.82) | data formatting | bytes 1245184
Async XLA Ops:
  0.0 0.7 %copy-start.6 = (s32[1,1,4,128]{3,2,1,0:T(4,128)S(1)}, s32[1,1,4,128]{3,2,1,0:T(4,128)}, u32[]{:S(2)}) copy-start(s32[1,1,4,128]{3,2,1,0:T(4,128)} %param.12) | copy-start | bytes 6148
  0.0 0.7 %copy-start.7 = (f32[19]{0:T(128)S(1)}, f32[19]{0:T(128)}, u32[]{:S(2)}) copy-start(f32[19]{0:T(128)} %refs_1_.1) | copy-start | bytes 232
  0.7 1.1 %copy-start = (f32[19,4,16,128]{3,2,1,0:T(8,128)S(1)}, f32[19,4,16,128]{3,2,1,0:T(8,128)}, u32[]{:S(2)}) copy-start(f32[19,4,16,128]{3,2,1,0:T(8,128)} %refs_0_.1) | copy-start | bytes 1867780
  1.8 0.8 %copy-start.1 = (s32[1,1,9,1024]{3,1,2,0:T(1,128)S(1)}, s32[1,1,9,1024]{3,1,2,0:T(1,128)}, u32[]{:S(2)}) copy-start(s32[1,1,9,1024]{3,1,2,0:T(1,128)} %param.13) | copy-start | bytes 110596
  2.5 0.8 %copy-start.2 = (s32[1,1,9,1024]{3,1,2,0:T(1,128)S(1)}, s32[1,1,9,1024]{3,1,2,0:T(1,128)}, u32[]{:S(2)}) copy-start(s32[1,1,9,1024]{3,1,2,0:T(1,128)} %param.14) | copy-start | bytes 110596
  3.3 0.8 %copy-start.3 = (f32[1,1,9,1024]{3,1,2,0:T(1,128)S(1)}, f32[1,1,9,1024]{3,1,2,0:T(1,128)}, u32[]{:S(2)}) copy-start(f32[1,1,9,1024]{3,1,2,0:T(1,128)} %param.15) | copy-start | bytes 110596
  4.1 0.8 %copy-start.4 = (s32[64,128]{1,0:T(8,128)S(1)}, s32[64,128]{1,0:T(8,128)}, u32[]{:S(2)}) copy-start(s32[64,128]{1,0:T(8,128)} %refs_2_.1) | copy-start | bytes 98308
  4.8 0.8 %copy-start.5 = (f32[4,1,1,2048]{3,2,1,0:T(1,128)S(1)}, f32[4,1,1,2048]{3,2,1,0:T(1,128)}, u32[]{:S(2)}) copy-start(f32[4,1,1,2048]{3,2,1,0:T(1,128)} %param.11) | copy-start | bytes 98308

commit v2 on v1

--- a/solution.py
+++ b/solution.py
@@ -176,6 +176,15 @@
 def kernel(
     devices_x,
     devices_z,
+    pops_hbm,
+    rates_hbm,
+    wall_hbm,
+    part_hbm,
+    list_hbm,
+    slot_hbm,
+    cell_hbm,
+    weight_hbm,
+    out_ref,
     pops_ref,
     rates_ref,
     wall_ref,
@@ -184,7 +193,7 @@
     slot_ref,
     cell_ref,
     weight_ref,
-    out_ref,
+    load_sem,
     stay,
     leave,
     arrive,
@@ -194,6 +203,7 @@
     plane_in,
     edge_out,
     edge_in,
+    corner_out,
     corner_in,
     coll,
     halo_x_out,
@@ -220,6 +230,22 @@
     for step in around:
         pl.semaphore_signal(barrier, inc=1, device_id=peer(*step), device_id_type=MESH)
 
+    loads = {}
+    for at, (name, source, target) in enumerate(
+        [
+            ("list", list_hbm, list_ref),
+            ("part", part_hbm, part_ref),
+            ("slot", slot_hbm, slot_ref),
+            ("weight", weight_hbm, weight_ref),
+            ("cell", cell_hbm, cell_ref),
+            ("wall", wall_hbm, wall_ref),
+            ("rates", rates_hbm, rates_ref),
+            ("pops", pops_hbm, pops_ref),
+        ]
+    ):
+        loads[name] = pltpu.make_async_copy(source, target, load_sem.at[at])
+        loads[name].start()
+
     count = [0]
 
     def send(source, target, step):
@@ -236,6 +262,8 @@
         copy.start()
         return copy
 
+    loads["list"].wait()
+    loads["part"].wait()
     lists = list_ref[...]
     lists8 = jnp.concatenate([lists, lists], axis=0)
     list_hi, list_lo = lists8 >> 7, lists8 & 127
@@ -282,8 +310,10 @@
             values[c, at] = got[c]
         return carry
 
+    loads["slot"].wait()
     lax.fori_loop(0, 9, first_pick, 0)
 
+    loads["wall"].wait()
     wall = jnp.where(
         (lax.broadcasted_iota(jnp.int32, (depth_z, 128), 1) == 0)
         | (lax.broadcasted_iota(jnp.int32, (depth_z, 128), 1) == 127),
@@ -298,11 +328,15 @@
     solid[PAD - 1 : PAD] = jnp.where(ends, 1, wall_ref[pl.ds(below, 1)])
     solid[PAD + depth_z : PAD + depth_z + 1] = jnp.where(ends, 1, wall_ref[pl.ds(above, 1)])
 
+    loads["weight"].wait()
+    loads["cell"].wait()
+    loads["rates"].wait()
+    loads["pops"].wait()
     for copy in migrations:
         copy.wait()
 
     def second_pick(j, carry):
-        at = pl.ds(pl.multiple_of(j * 8, 8), 8)
+        at = pl.ds(j * 8 if isinstance(j, int) else pl.multiple_of(j * 8, 8), 8)
         slots = slot_ref[at]
         hi, lo = slots >> 7, slots & 127
         got = [values[c, at] for c in range(4)]
@@ -316,7 +350,10 @@
         values[3, at] = scale
         return carry
 
-    lax.fori_loop(0, 9, second_pick, 0)
+    def outer_pick(n, carry):
+        return second_pick(jnp.where(n >= 4, n + 1, n), carry)
+
+    lax.fori_loop(0, 8, outer_pick, 0)
 
     def bucket(step_x, step_z):
         at = ((step_x + 1) * 3 + step_z + 1) * 8
@@ -338,7 +375,12 @@
         edge_out[s] = total.reshape(4, 8, 128)
         exchanges.append(send(edge_out.at[s], edge_in.at[s], (0, step)))
         for sx, step_x in enumerate(STEP):
-            exchanges.append(send(edge_out.at[s], corner_in.at[s * 2 + sx], (step_x, step)))
+            at = s * 2 + sx
+            row = 5 if step_x == 1 else 0
+            for c in range(4):
+                corner_out[at, c : c + 1] = total[c * 8 + row : c * 8 + row + 1]
+            exchanges.append(send(corner_out.at[at], corner_in.at[at], (step_x, step)))
+    second_pick(4, 0)
     got, cells = bucket(0, 0)
     force[...] = spread(got, cells >> 7, cells & 127, 64).reshape(4, 4, 16, 128)
     for copy in exchanges:
@@ -353,9 +395,9 @@
             for x in range(4):
                 row = edge_in[s, c, x + 1 : x + 2]
                 if x == 0:
-                    row = row + corner_in[s * 2, c, 5:6]
+                    row = row + corner_in[s * 2, c : c + 1]
                 if x == 3:
-                    row = row + corner_in[s * 2 + 1, c, 0:1]
+                    row = row + corner_in[s * 2 + 1, c : c + 1]
                 force[c, x, z : z + 1] = force[c, x, z : z + 1] + row
 
     rates = [rates_ref[k] for k in range(19)]
@@ -386,6 +428,33 @@
             halos.append(
                 send(halo_z_out.at[s, n], halo_c_in.at[s * 2 + sx], (STEP[sx], STEP[s]))
             )
+    def stream(late):
+        for q in range(19):
+            step_x, step_y, step_z = VELOCITIES[q]
+            for half in range(2):
+                chosen = [
+                    x
+                    for x in range(4)
+                    if late
+                    == (
+                        (step_x, x) in ((1, 0), (-1, 3)) or (step_z, half) in ((1, 0), (-1, 1))
+                    )
+                ]
+                if not chosen:
+                    continue
+                at = PAD + 8 * half
+                blocked = solid[at - step_z : at - step_z + 8]
+                if step_y:
+                    blocked = pltpu.roll(blocked, step_y % 128, 1)
+                for x in chosen:
+                    moved = coll[q, 1 + x - step_x, at - step_z : at - step_z + 8]
+                    if step_y:
+                        moved = pltpu.roll(moved, step_y % 128, 1)
+                    out_ref[q, x, 8 * half : 8 * half + 8] = jnp.where(
+                        blocked > 0, coll[OPPOSITE[q], 1 + x, at : at + 8], moved
+                    )
+
+    stream(False)
     for copy in halos:
         copy.wait()
     for s in range(2):
@@ -400,18 +469,7 @@
             x = 3 if sx == 0 else 0
             coll[q, 0 if sx == 0 else 5, z : z + 1] = halo_c_in[s * 2 + sx, x : x + 1]
 
-    for q in range(19):
-        step_x, step_y, step_z = VELOCITIES[q]
-        blocked = solid[PAD - step_z : PAD - step_z + 16]
-        if step_y:
-            blocked = pltpu.roll(blocked, step_y % 128, 1)
-        for x in range(4):
-            moved = coll[q, 1 + x - step_x, PAD - step_z : PAD - step_z + 16]
-            if step_y:
-                moved = pltpu.roll(moved, step_y % 128, 1)
-            out_ref[q, x] = jnp.where(
-                blocked > 0, coll[OPPOSITE[q], 1 + x, PAD : PAD + 16], moved
-            )
+    stream(True)
 
 
 def solution(mesh):
@@ -419,14 +477,23 @@
 
     def body(pops, rates, wall, particles, lists, slot, cell, weight):
         vmem = pl.BlockSpec(memory_space=pltpu.VMEM)
-        smem = pl.BlockSpec(memory_space=pltpu.SMEM)
+        hbm = pl.BlockSpec(memory_space=pltpu.HBM)
         f32 = jnp.float32
         return pl.pallas_call(
             lambda *refs: kernel(devices_x, devices_z, *refs),
             out_shape=jax.ShapeDtypeStruct(pops.shape, f32),
-            in_specs=[vmem, smem] + [vmem] * 6,
+            in_specs=[hbm] * 8,
             out_specs=vmem,
             scratch_shapes=[
+                pltpu.VMEM(pops.shape, f32),
+                pltpu.SMEM(rates.shape, f32),
+                pltpu.VMEM(wall.shape, jnp.int32),
+                pltpu.VMEM((64, 128), f32),
+                pltpu.VMEM((4, 128), jnp.int32),
+                pltpu.VMEM((72, 128), jnp.int32),
+                pltpu.VMEM((72, 128), jnp.int32),
+                pltpu.VMEM((72, 128), f32),
+                pltpu.SemaphoreType.DMA((8,)),
                 pltpu.VMEM((4, 16, 128), f32),
                 pltpu.VMEM((4, 8, 128), f32),
                 pltpu.VMEM((4, 8, 128), f32),
@@ -436,7 +503,8 @@
                 pltpu.VMEM((2, 4, 16, 128), f32),
                 pltpu.VMEM((2, 4, 8, 128), f32),
                 pltpu.VMEM((2, 4, 8, 128), f32),
-                pltpu.VMEM((4, 4, 8, 128), f32),
+                pltpu.VMEM((4, 4, 128), f32),
+                pltpu.VMEM((4, 4, 128), f32),
                 pltpu.VMEM((19, 6, 32, 128), f32),
                 pltpu.VMEM((2, 5, 16, 128), f32),
                 pltpu.VMEM((2, 5, 16, 128), f32),
@@ -448,7 +516,7 @@
                 pltpu.SemaphoreType.DMA((20,)),
             ],
             compiler_params=pltpu.CompilerParams(
-                collective_id=0, has_side_effects=True, vmem_limit_bytes=48 * 1024 * 1024
+                collective_id=0, has_side_effects=True, vmem_limit_bytes=56000 * 1024
             ),
         )(
             pops,

time: 28.2 us -> 23.5 us (0.83); the launches traced: 27.7 us -> 23.4 us
  local copies, waits for them, and re-layouts: 6.4 us -> 1.96 us
    unnamed x17 -> x1, local copies, waits for them, and re-layouts: 6.4 us -> 1.96 us
where the time goes in v2:
time: 23.5 us; the launch traced here: 23.4 us
  Pallas kernels  21.4 us (91%)
  local copies, waits for them, and re-layouts  1.96 us (8%)
    pallas_call x1, Pallas kernels, body(): pl.pallas_call(lambda *refs: kernel(devices_x, devices_z, *refs), out_sha...  21.4 us
    unnamed x1, local copies, waits for them, and re-layouts  1.96 us

profile of v2, /device:TPU:0, one launch (start us, length us, event | category | flops | bytes accessed | tf_op | source)
XLA Modules:
  0.0 23.4 jit_solution(16994247674235130370)
XLA Ops:
  0.0 21.4 %shard_map.82 = f32[19,4,16,128]{3,2,1,0:T(8,128)} custom-call(f32[19,4,16,128]{3,2,1,0:T(8,128)} %refs_0_.1, f32[19]{0:T(128)} %refs_1_.1, s32[64,128]{1,0:T(8,128)} %refs_2_.1, f32[64,128]{1,0:T(8,128)} %bitcast.8, s32[4,128]{1,0:T(4,128)} %bitcast.9, s32[72,128]{1,0:T(8,128)} %bitcast.5, s32[72,128]{1,0:T(8,128)} %bitcast.6, f32[72,128]{1,0:T(8,128)} %bitcast.7), custom_call_target="tpu_custom_call" | custom-call | tf_op jit(solution)/shard_map/pallas_call | solution.py:482
  21.4 2.0 %copy.10 = f32[19,4,16,128]{3,2,1,0:T(8,128)} copy(f32[19,4,16,128]{3,2,1,0:T(8,128)} %shard_map.82) | data formatting | bytes 1245184

commit v3 on v2

--- a/solution.py
+++ b/solution.py
@@ -481,7 +481,7 @@
         f32 = jnp.float32
         return pl.pallas_call(
             lambda *refs: kernel(devices_x, devices_z, *refs),
-            out_shape=jax.ShapeDtypeStruct(pops.shape, f32),
+            out_shape=pltpu.VMEM(pops.shape, f32),
             in_specs=[hbm] * 8,
             out_specs=vmem,
             scratch_shapes=[

time: 23.5 us -> 21.6 us (0.919)
  local copies, waits for them, and re-layouts: 1.96 us -> 0.83 us
  Pallas kernels: 21.4 us -> 20.6 us
    unnamed x1, local copies, waits for them, and re-layouts: 1.96 us -> 0.83 us
    pallas_call x1, Pallas kernels: 21.4 us -> 20.6 us  [body(): pl.pallas_call(lambda *refs: kernel(devices_x, devices_z, *refs), out_sha...]
where the time goes in v3:
time: 21.6 us; the launch traced here: 21.4 us
  Pallas kernels  20.6 us (95%)
  local copies, waits for them, and re-layouts  0.83 us (4%)
    pallas_call x1, Pallas kernels, body(): pl.pallas_call(lambda *refs: kernel(devices_x, devices_z, *refs), out_sha...  20.6 us
    unnamed x1, local copies, waits for them, and re-layouts  0.83 us

profile of v3, /device:TPU:0, one launch (start us, length us, event | category | flops | bytes accessed | tf_op | source)
XLA Modules:
  0.0 21.4 jit_solution(17087447568038317529)
XLA Ops:
  0.0 20.6 %shard_map.82 = f32[19,4,16,128]{3,2,1,0:T(8,128)S(1)} custom-call(f32[19,4,16,128]{3,2,1,0:T(8,128)} %refs_0_.1, f32[19]{0:T(128)} %refs_1_.1, s32[64,128]{1,0:T(8,128)} %refs_2_.1, f32[64,128]{1,0:T(8,128)} %bitcast.8, s32[4,128]{1,0:T(4,128)} %bitcast.9, s32[72,128]{1,0:T(8,128)} %bitcast.5, s32[72,128]{1,0:T(8,128)} %bitcast.6, f32[72,128]{1,0:T(8,128)} %bitcast.7), custom_call_target="tpu_custom_call" | custom-call | tf_op jit(solution)/shard_map/pallas_call | solution.py:482
  20.6 0.8 %copy.10 = f32[19,4,16,128]{3,2,1,0:T(8,128)} copy(f32[19,4,16,128]{3,2,1,0:T(8,128)S(1)} %shard_map.82) | data formatting | bytes 1245184

commit v4 on v3

--- a/solution.py
+++ b/solution.py
@@ -210,6 +210,7 @@
     halo_x_in,
     halo_z_out,
     halo_z_in,
+    halo_c_out,
     halo_c_in,
     solid,
     send_sem,
@@ -362,10 +363,6 @@
 
     exchanges = []
     for s, step in enumerate(STEP):
-        got, cells = bucket(step, 0)
-        plane_out[s] = spread(got, (cells >> 7) & 15, cells & 127, 16).reshape(4, 16, 128)
-        exchanges.append(send(plane_out.at[s], plane_in.at[s], (step, 0)))
-    for s, step in enumerate(STEP):
         total = None
         for step_x in (-1, 0, 1):
             got, cells = bucket(step_x, step)
@@ -380,6 +377,10 @@
             for c in range(4):
                 corner_out[at, c : c + 1] = total[c * 8 + row : c * 8 + row + 1]
             exchanges.append(send(corner_out.at[at], corner_in.at[at], (step_x, step)))
+    for s, step in enumerate(STEP):
+        got, cells = bucket(step, 0)
+        plane_out[s] = spread(got, (cells >> 7) & 15, cells & 127, 16).reshape(4, 16, 128)
+        exchanges.append(send(plane_out.at[s], plane_in.at[s], (step, 0)))
     second_pick(4, 0)
     got, cells = bucket(0, 0)
     force[...] = spread(got, cells >> 7, cells & 127, 64).reshape(4, 4, 16, 128)
@@ -419,15 +420,15 @@
             s = 0 if x == 3 else 1
             for n, q in enumerate(ALONG_X[s]):
                 halo_x_out[s, n] = done[q]
+            for sz in range(2):
+                q = VELOCITIES.index((STEP[s], 0, STEP[sz]))
+                z = 15 if sz == 0 else 0
+                at = sz * 2 + s
+                halo_c_out[at, 0:1] = done[q][z : z + 1]
+                halos.append(send(halo_c_out.at[at], halo_c_in.at[at], (STEP[s], STEP[sz])))
             halos.append(send(halo_x_out.at[s], halo_x_in.at[s], (STEP[s], 0)))
     for s in range(2):
         halos.append(send(halo_z_out.at[s], halo_z_in.at[s], (0, STEP[s])))
-        for sx in range(2):
-            q = VELOCITIES.index((STEP[sx], 0, STEP[s]))
-            n = ALONG_Z[s].index(q)
-            halos.append(
-                send(halo_z_out.at[s, n], halo_c_in.at[s * 2 + sx], (STEP[sx], STEP[s]))
-            )
     def stream(late):
         for q in range(19):
             step_x, step_y, step_z = VELOCITIES[q]
@@ -466,8 +467,7 @@
                 coll[q, 1 + x, z : z + 1] = halo_z_in[s, n, x : x + 1]
         for sx in range(2):
             q = VELOCITIES.index((STEP[sx], 0, STEP[s]))
-            x = 3 if sx == 0 else 0
-            coll[q, 0 if sx == 0 else 5, z : z + 1] = halo_c_in[s * 2 + sx, x : x + 1]
+            coll[q, 0 if sx == 0 else 5, z : z + 1] = halo_c_in[s * 2 + sx, 0:1]
 
     stream(True)
 
@@ -511,6 +511,7 @@
                 pltpu.VMEM((2, 5, 8, 128), f32),
                 pltpu.VMEM((2, 5, 8, 128), f32),
                 pltpu.VMEM((4, 8, 128), f32),
+                pltpu.VMEM((4, 8, 128), f32),
                 pltpu.VMEM((32, 128), jnp.int32),
                 pltpu.SemaphoreType.DMA((20,)),
                 pltpu.SemaphoreType.DMA((20,)),

time: 21.6 us -> 21.4 us (level)
  no operation moved by 1% of the time
where the time goes in v4:
time: 21.4 us; the launch traced here: 21.3 us
  Pallas kernels  20.4 us (95%)
  local copies, waits for them, and re-layouts  0.83 us (4%)
    pallas_call x1, Pallas kernels, body(): pl.pallas_call(lambda *refs: kernel(devices_x, devices_z, *refs), out_sha...  20.4 us
    unnamed x1, local copies, waits for them, and re-layouts  0.83 us

profile of v4, /device:TPU:0, one launch (start us, length us, event | category | flops | bytes accessed | tf_op | source)
XLA Modules:
  0.0 21.3 jit_solution(17218670415964210110)
XLA Ops:
  0.0 20.4 %shard_map.82 = f32[19,4,16,128]{3,2,1,0:T(8,128)S(1)} custom-call(f32[19,4,16,128]{3,2,1,0:T(8,128)} %refs_0_.1, f32[19]{0:T(128)} %refs_1_.1, s32[64,128]{1,0:T(8,128)} %refs_2_.1, f32[64,128]{1,0:T(8,128)} %bitcast.8, s32[4,128]{1,0:T(4,128)} %bitcast.9, s32[72,128]{1,0:T(8,128)} %bitcast.5, s32[72,128]{1,0:T(8,128)} %bitcast.6, f32[72,128]{1,0:T(8,128)} %bitcast.7), custom_call_target="tpu_custom_call" | custom-call | tf_op jit(solution)/shard_map/pallas_call | solution.py:482
  20.5 0.8 %copy.10 = f32[19,4,16,128]{3,2,1,0:T(8,128)} copy(f32[19,4,16,128]{3,2,1,0:T(8,128)S(1)} %shard_map.82) | data formatting | bytes 1245184
